TPU v7x, 256 devices: a whole 4x4x8 slice. The times are simulated.
256 devices in a mesh: src: 2 (over x_lo), lat: 128 (over z, x_hi, y, core).
Axes of the slice: x: 4 (x_hi: 2, x_lo: 2; x = x_hi * 2 + x_lo), y: 4, z: 8, core: 2. Of those that a mesh axis runs over, the one named last changes fastest.
Arguments:
- resid: bfloat16 [2, 512, 4096], P('src', 'lat'), may hold values from -6 to 6
- token_ids: int32 [512], replicated, may hold values from 0 to 511, each once
- enc_weight: bfloat16 [2, 4096, 32768], P('src', None, 'lat'), may hold values from -0.09375 to 0.09375
- enc_bias: float32 [2, 32768], P('src', 'lat'), may hold values from -3.2 to -1.8
- threshold: float32 [2, 32768], P('src', 'lat'), may hold values from 0.1 to 1
- dec_self: bfloat16 [2, 32768, 4096], P('src', 'lat'), may hold values from -0.375 to 0.375
- dec_cross: bfloat16 [32768, 4096], P('lat'), may hold values from -0.375 to 0.375
Outputs:
- recon: bfloat16 [2, 512, 4096], P('src', 'lat')
Inputs may be any that keep to these rules, and one draw needn't show every extreme that they name: token_ids names every pool row exactly once.
All inputs are finite; a program needn't handle non-finite values.
Results may differ from a plain program's by a relative error of at most 0.005.
Values may be sent and summed in bfloat16 or wider, within the bound.
A program may use at most 128 MiB of HBM per device.

v0:
```python
import jax
import jax.numpy as jnp
from jax import lax
from jax.sharding import PartitionSpec as P


def shifted(block, axis, distance):
    devices = range(lax.axis_size(axis))
    route = [(i - distance, i) for i in devices if i - distance in devices]
    return lax.ppermute(block, axis, route)


def on_device(resid, token_ids, enc_weight, enc_bias, threshold, dec_self, dec_cross):
    rows = resid[0]
    weight = enc_weight[0]
    bias = enc_bias[0]
    thresh = threshold[0]
    own_dec = dec_self[0]
    pre = (
        jnp.dot(
            lax.all_gather(rows, "lat", axis=0, tiled=True),
            weight,
            preferred_element_type=jnp.float32,
        )
        + bias
    )
    pooled = (pre * jnp.clip((pre - thresh) / 0.1, 0.0, 1.0)).astype(jnp.bfloat16)
    codes = jnp.take(pooled, token_ids, axis=0)
    earlier = shifted(codes, "src", 1)
    total = jnp.dot(codes, own_dec, preferred_element_type=jnp.float32)
    summed = lax.psum_scatter(
        total + jnp.dot(earlier, dec_cross, preferred_element_type=jnp.float32),
        "lat",
        scatter_dimension=0,
        tiled=True,
    )
    return summed.astype(jnp.bfloat16)[None]


def solution(mesh):
    in_specs = (
        P("src", "lat", None),
        P(),
        P("src", None, "lat"),
        P("src", "lat"),
        P("src", "lat"),
        P("src", "lat", None),
        P("lat", None),
    )
    out_specs = P("src", "lat", None)
    return jax.shard_map(
        on_device, mesh=mesh, in_specs=in_specs, out_specs=out_specs, check_vma=False
    )
```

profile of v0, /device:TPU:2, one launch (start us, length us, event | category | flops | bytes accessed | tf_op | source)
XLA Modules:
  0.0 913.4 jit_solution(5475614872465730049)
XLA Ops:
  6.5 0.0 copy-start
  6.5 0.0 all-gather.3.cloned.1.call-start
  6.5 1.6 copy.9
  8.1 0.0 all-gather.3.cloned.1.call-update
  8.1 1.3 dynamic-slice
  10.1 0.7 compare_select_fusion
  10.8 0.7 compare_and_fusion
  11.4 131.1 %all-gather.3.cloned.1.call-done = bf16[1,512,4096]{2,0,1:T(2,128)(2,1)} async-done(((bf16[1,4,4096]{2,0,1:T(2,128)(2,1)}), bf16[1,512,4096]{2,0,1:T(2,128)(2,1)}) %all-gather.3.cloned.1.call-update) | async-done | bytes 4194320 | tf_op jit(solution)/shard_map/all_gather | solution.py:21
  142.5 8.6 multiply_convert_fusion
  151.1 2.0 gather_fusion
  153.1 0.1 broadcast_select_fusion
  153.2 0.0 copy-start.1
  153.3 1.4 collective-permute-start
  154.7 0.0 copy-done
  154.7 1.3 fusion.3
  156.0 7.8 collective-permute-done
  163.8 0.0 copy-done.1
  163.8 4.5 convolution_add_fusion
  168.2 736.8 %all-reduce.2 = bf16[512,4096]{1,0:T(8,128)(2,1)} all-reduce(f32[512,4096]{1,0:T(8,128)} %convolution_add_fusion), channel_id=3, replica_groups=mesh['src'=2,'lat'=128] {'lat'}, use_global_device_ids=true, to_apply=%region_0.1.clone | all-reduce | flops 2097152 | bytes 12582912
  905.1 1.5 fusion.15
  (1 shorter events, 0.0 us)
Async XLA Ops:
  6.5 148.2 %copy-start = (bf16[1,256,4096]{2,1,0:T(8,128)(2,1)S(1)}, bf16[1,256,4096]{2,1,0:T(8,128)(2,1)}, u32[]{:S(2)}) copy-start(bf16[1,256,4096]{2,1,0:T(8,128)(2,1)} %param.12) | copy-start | bytes 6291460
  6.5 136.0 %all-gather.3.cloned.1.call-start = ((), (), s32[]{:S(2)}) async-start(), calls=%async_computation | async-start | bytes 8454144 | tf_op jit(solution)/shard_map/all_gather | solution.py:21
  153.2 10.5 %copy-start.1 = (bf16[256,4096]{1,0:T(8,128)(2,1)S(1)}, bf16[256,4096]{1,0:T(8,128)(2,1)}, u32[]{:S(2)}) copy-start(bf16[256,4096]{1,0:T(8,128)(2,1)} %param.13) | copy-start | bytes 6291460
  153.3 10.5 %collective-permute-start = (bf16[512,256]{1,0:T(8,128)(2,1)S(1)}, bf16[512,256]{1,0:T(8,128)(2,1)S(1)}, u32[]{:S(2)}, u32[]{:S(2)}) collective-permute-start(bf16[512,256]{1,0:T(8,128)(2,1)S(1)} %broadcast_select_fusion), channel_id=1, source_target_pairs={{0,128},{1,129},{2,130},{3,131},{4,132},{5,133},{6,134},{7,135},{8... | collective-permute-start | bytes 786440 | tf_op jit(solution)/shard_map/ppermute | solution.py:10
Sparse Core Ops, SparseCore 0:
  11.1 131.3 all-gather.2
where the time goes:
time: 914 us; the launch traced here: 913 us
  blocking collectives  737 us (81%)
  waiting for transfers between devices  139 us (15%)
  matrix products  14.4 us (2%)
  between operations  14.1 us (2%)
    unnamed x1, blocking collectives  737 us
    all_gather x1, waiting for transfers between devices, on_device(): lax.all_gather(rows, 'lat', axis=0, tiled=True)  131 us
  transfers between devices with their start and end apart: 2, of which 2 were waited for; matrix products, arithmetic and copies ran while one was open for 0% of the time, Pallas kernels for 0%

commit v1 on v0

v1 whole, which is shorter than its diff:
```python
import jax
import jax.numpy as jnp
from jax import lax
from jax.experimental import pallas as pl
from jax.experimental.pallas import tpu as pltpu
from jax.sharding import PartitionSpec as P

MESH = pl.DeviceIdType.MESH
BF16, F32 = jnp.bfloat16, jnp.float32

NZ, NX, NY = 8, 2, 4
ROWS = 4
D, LAT = 4096, 256
PLANE = NZ * NX * NY * ROWS
QUARTER = D // 4
XFIRST = 384
TILE = 512
TILES = D // TILE
Y_TILES = (0, 3, 6)
Z_GROUPS = ((0, 2), (2, 4), (4, 6), (6, 8))
Z_ORDER = (0, 1, 7, 2, 6, 3, 5, 4)


def kernel(
    ids,
    resid,
    bias,
    thresh,
    enc_hbm,
    own_hbm,
    cross_hbm,
    out,
    blocks,
    rows,
    enc,
    own_dec,
    cross_dec,
    bias2,
    thresh2,
    codes,
    earlier,
    select,
    mixed,
    mixed_cross,
    part,
    send1,
    half,
    send2,
    send3,
    last,
    got_x1,
    got_y2,
    got_y1,
    got_x2,
    got_z,
    local_sem,
    core_send,
    core_recv,
    code_send,
    code_recv,
    z_send,
    z_recv,
    cy_send,
    cy_recv,
    cx_send,
    cx_recv,
    bx_send,
    bx_recv,
    by_send,
    by_recv,
    s1_send,
    s1_recv,
    s2_send,
    s2_recv,
    s3_send,
    s3_recv,
):
    src = lax.axis_index("src")
    lat = lax.axis_index("lat")
    core = lax.rem(lat, 2)
    y = lax.rem(lat // 2, NY)
    x = lax.rem(lat // (2 * NY), NX)
    z = lat // (2 * NY * NX)

    def at(z, x, y, core):
        return (src, ((z * NX + x) * NY + y) * 2 + core)

    def zp(dz):
        return lax.rem(z + NZ - dz, NZ)

    def zn(dz):
        return lax.rem(z + dz, NZ)

    def yn(dy):
        return lax.rem(y + dy, NY)

    other_core = at(z, x, y, 1 - core)
    other_src = (1 - src, lat)
    other_x = at(z, 1 - x, y, core)

    def remote(src_ref, dst_ref, send, recv, device):
        return pltpu.make_async_remote_copy(
            src_ref=src_ref,
            dst_ref=dst_ref,
            send_sem=send,
            recv_sem=recv,
            device_id=device,
            device_id_type=MESH,
        )

    started = []

    def go(copy):
        copy.start()
        started.append(copy)

    locals_ = [
        pltpu.make_async_copy(enc_hbm.at[0], enc.at[core], local_sem.at[0]),
        pltpu.make_async_copy(own_hbm.at[0], own_dec.at[core], local_sem.at[1]),
        pltpu.make_async_copy(cross_hbm, cross_dec.at[core], local_sem.at[2]),
    ]
    for copy in locals_:
        copy.start()

    mine = resid[0].astype(F32)
    blocks[z, x, y] = jnp.concatenate(
        [mine[:, q * QUARTER : (q + 1) * QUARTER] for q in range(4)], axis=0
    ).astype(BF16)

    bias2[core] = bias[...]
    thresh2[core] = thresh[...]

    barrier = pltpu.get_barrier_semaphore()
    peers = [at(zn(o), x, y, core) for o in range(1, NZ)]
    peers += [at(z, x, yn(o), core) for o in range(1, NY)]
    peers += [other_x, other_core, other_src]
    for peer in peers:
        pl.semaphore_signal(barrier, inc=1, device_id=peer, device_id_type=MESH)
    pl.semaphore_wait(barrier, len(peers))

    def z_copy(o):
        ref = blocks.at[z, x, y]
        return remote(ref, ref, z_send.at[o], z_recv.at[o], at(zn(o), x, y, core))

    for o in Z_ORDER[1:]:
        go(z_copy(o))

    b_cols, c_cols = pl.ds(0, XFIRST), pl.ds(XFIRST, QUARTER - XFIRST)

    def cy_copy(dz, o):
        ref = blocks.at[zp(dz), x, y, :, c_cols]
        return remote(
            ref, ref, cy_send.at[dz, o], cy_recv.at[dz, o], at(z, x, yn(o), core)
        )

    def bx_copy(dz):
        ref = blocks.at[zp(dz), x, y, :, b_cols]
        return remote(ref, ref, bx_send.at[dz], bx_recv.at[dz], other_x)

    def cx_copy(dz):
        ref = blocks.at[zp(dz), x, :, :, c_cols]
        return remote(ref, ref, cx_send.at[dz], cx_recv.at[dz], other_x)

    def by_copy(dz, o):
        ref = blocks.at[zp(dz), :, y, :, b_cols]
        return remote(
            ref, ref, by_send.at[dz, o], by_recv.at[dz, o], at(z, x, yn(o), core)
        )

    def second(dz):
        if dz:
            z_copy(dz).wait_recv()
        for o in (1, 3, 2):
            go(cy_copy(dz, o))
        go(bx_copy(dz))

    def third(dz):
        bx_copy(dz).wait_recv()
        for o in (1, 3, 2):
            go(by_copy(dz, o))
        for o in (1, 3, 2):
            cy_copy(dz, o).wait_recv()
        go(cx_copy(dz))

    second(0)

    core_copies = [
        remote(bias, bias2.at[core], core_send.at[3], core_recv.at[3], other_core),
        remote(
            thresh, thresh2.at[core], core_send.at[4], core_recv.at[4], other_core
        ),
        remote(
            enc_hbm.at[0], enc.at[core], core_send.at[0], core_recv.at[0], other_core
        ),
        remote(
            own_hbm.at[0],
            own_dec.at[core],
            core_send.at[1],
            core_recv.at[1],
            other_core,
        ),
    ]
    for copy in core_copies:
        go(copy)
    cross_copy = remote(
        cross_hbm, cross_dec.at[core], core_send.at[2], core_recv.at[2], other_core
    )

    @pl.when(src == 1)
    def _():
        cross_copy.start()

    shape = (2 * PLANE, 2 * PLANE)
    j = lax.broadcasted_iota(jnp.int32, shape, 0)
    plane, within = j // PLANE, j % PLANE
    pool = (within // ROWS) * (2 * ROWS) + plane * ROWS + within % ROWS
    named = (jnp.broadcast_to(ids[...], shape) == pool).astype(F32).astype(BF16)
    i = lax.broadcasted_iota(jnp.int32, (PLANE, 2 * PLANE), 0)
    t = lax.broadcasted_iota(jnp.int32, (PLANE, 2 * PLANE), 1)
    ir, iz, iy, ix = i % 4, (i // 4) % NZ, (i // (4 * NZ)) % NY, i // (4 * NZ * NY)
    token = (((iz * NX + ix) * NY + iy) * 2 + core) * ROWS + ir
    order = (t == token).astype(F32).astype(BF16)
    select[...] = lax.dot_general(
        order, named, (((1,), (1,)), ((), ())), preferred_element_type=F32
    ).astype(BF16)

    lag = 2
    for n, dz in enumerate(Z_ORDER):
        if n:
            second(dz)
        if n >= lag:
            third(Z_ORDER[n - lag])
    for dz in Z_ORDER[NZ - lag :]:
        third(dz)

    def unpack(dz):
        zz = zp(dz)
        for xx in range(NX):
            four = [blocks[zz, xx, yy].astype(F32) for yy in range(NY)]
            start = pl.multiple_of((zz * NX + xx) * (NY * ROWS), NY * ROWS)
            for q in range(4):
                rows[pl.ds(start, NY * ROWS), q * QUARTER : (q + 1) * QUARTER] = (
                    jnp.concatenate([b[4 * q : 4 * q + 4] for b in four], axis=0)
                ).astype(BF16)

    for dz in Z_ORDER:
        for o in (1, 3, 2):
            by_copy(dz, o).wait_recv()
        cx_copy(dz).wait_recv()
        unpack(dz)

    locals_[0].wait()
    for copy in core_copies[:3]:
        copy.wait_recv()
    for h in range(2):
        pre = jnp.dot(rows[...], enc[h], preferred_element_type=F32) + bias2[h]
        gate = jnp.clip((pre - thresh2[h]) / 0.1, 0.0, 1.0)
        codes[core, :, h * LAT : (h + 1) * LAT] = (pre * gate).astype(BF16)

    code_copy = remote(
        codes.at[core], codes.at[core], code_send.at[0], code_recv.at[0], other_core
    )
    go(code_copy)
    over = remote(
        codes.at[core], earlier.at[core], code_send.at[1], code_recv.at[1], other_src
    )
    on = remote(
        earlier.at[core], earlier.at[core], code_send.at[2], code_recv.at[2], other_core
    )

    @pl.when(src == 0)
    def _():
        over.start()

    code_copy.wait_recv()

    def permuted(ref):
        return jnp.dot(
            select[...], ref[...].reshape(2 * PLANE, 2 * LAT), preferred_element_type=F32
        ).astype(BF16)

    mixed[...] = permuted(codes)
    locals_[1].wait()
    core_copies[3].wait_recv()
    locals_[2].wait()

    @pl.when(src == 1)
    def _():
        over.wait_recv()
        on.start()
        cross_copy.wait_recv()
        on.wait_recv()
        mixed_cross[...] = permuted(earlier)

    def decode(n):
        cols = slice(n * TILE, (n + 1) * TILE)
        total = jnp.zeros((PLANE, TILE), F32)
        for h in range(2):
            total += jnp.dot(
                mixed[:, h * LAT : (h + 1) * LAT],
                own_dec[h, :, cols],
                preferred_element_type=F32,
            )
        part[n] = total.reshape(NX, NY, NZ * ROWS, TILE)

        @pl.when(src == 1)
        def _():
            total = part[n].reshape(PLANE, TILE)
            for h in range(2):
                total += jnp.dot(
                    mixed_cross[:, h * LAT : (h + 1) * LAT],
                    cross_dec[h, :, cols],
                    preferred_element_type=F32,
                )
            part[n] = total.reshape(NX, NY, NZ * ROWS, TILE)

        send1[n] = part[n].astype(BF16)

    def y1_copy(n, o):
        return remote(
            send1.at[n, :, yn(o)],
            got_y1.at[n, o],
            s1_send.at[n, o],
            s1_recv.at[n, o],
            at(z, x, yn(o), core),
        )

    def x1_copy(n):
        return remote(
            send1.at[n, 1 - x], got_x1.at[n], s1_send.at[n, 0], s1_recv.at[n, 0], other_x
        )

    def y2_copy(n, o):
        return remote(
            send2.at[n, yn(o)],
            got_y2.at[n, o],
            s2_send.at[n, o],
            s2_recv.at[n, o],
            at(z, x, yn(o), core),
        )

    def x2_copy(n):
        return remote(
            send2.at[n, 1 - x], got_x2.at[n], s2_send.at[n, 0], s2_recv.at[n, 0], other_x
        )

    def z3_copy(g, o):
        first, end = Z_GROUPS[g]
        return remote(
            send3.at[zn(o), pl.ds(first, end - first)],
            got_z.at[o, pl.ds(first, end - first)],
            s3_send.at[g, o],
            s3_recv.at[g, o],
            at(zn(o), x, y, core),
        )

    def stage1(n):
        decode(n)
        if n in Y_TILES:
            for o in (1, 3, 2):
                go(y1_copy(n, o))
        else:
            go(x1_copy(n))

    def stage2(n):
        if n in Y_TILES:
            for o in (1, 3, 2):
                y1_copy(n, o).wait_recv()
            total = part[n, :, y]
            for o in (1, 3, 2):
                total += got_y1[n, o].astype(F32)
            half[n, 0:NX] = total
            send2[n, 0:NX] = total.astype(BF16)
            go(x2_copy(n))
        else:
            x1_copy(n).wait_recv()
            total = part[n, x] + got_x1[n].astype(F32)
            half[n] = total
            send2[n] = total.astype(BF16)
            for o in (1, 3, 2):
                go(y2_copy(n, o))

    def stage3(n):
        if n in Y_TILES:
            x2_copy(n).wait_recv()
            total = half[n, x] + got_x2[n].astype(F32)
        else:
            for o in (1, 3, 2):
                y2_copy(n, o).wait_recv()
            total = half[n, y]
            for o in (1, 3, 2):
                total += got_y2[n, o].astype(F32)
        step = TILE // 4
        for zz in range(NZ):
            block = jnp.concatenate(
                [
                    total[zz * ROWS : (zz + 1) * ROWS, q * step : (q + 1) * step]
                    for q in range(4)
                ],
                axis=0,
            )
            last[zz, n] = block
            send3[zz, n] = block.astype(BF16)
        for g, (_, end) in enumerate(Z_GROUPS):
            if n == end - 1:
                for o in Z_ORDER[:0:-1]:
                    go(z3_copy(g, o))

    def finish(g):
        first, end = Z_GROUPS[g]
        for o in range(1, NZ):
            z3_copy(g, o).wait_recv()
        step = TILE // 4
        for n in range(first, end):
            total = last[z, n]
            for o in range(1, NZ):
                total += got_z[o, n].astype(F32)
            for q in range(4):
                out[0, :, n * TILE + q * step : n * TILE + (q + 1) * step] = total[
                    q * ROWS : (q + 1) * ROWS
                ].astype(BF16)

    for n in range(TILES):
        stage1(n)
    for n in range(TILES + 2):
        if n < TILES:
            stage2(n)
        if n >= 2:
            stage3(n - 2)
    for g in range(len(Z_GROUPS)):
        finish(g)

    for copy in started:
        copy.wait_send()

    @pl.when(src == 0)
    def _():
        over.wait_send()

    @pl.when(src == 1)
    def _():
        cross_copy.wait_send()
        on.wait_send()


def on_device(
    resid, token_ids, enc_weight, enc_bias, threshold, dec_self, dec_cross
):
    vmem = pl.BlockSpec(memory_space=pltpu.VMEM)
    hbm = pl.BlockSpec(memory_space=pl.ANY)
    dma = pltpu.SemaphoreType.DMA
    scratch = [
        pltpu.VMEM((NZ, NX, NY, 16, QUARTER), BF16),
        pltpu.VMEM((PLANE, D), BF16),
        pltpu.VMEM((2, D, LAT), BF16),
        pltpu.VMEM((2, LAT, D), BF16),
        pltpu.VMEM((2, LAT, D), BF16),
        pltpu.VMEM((2, 1, LAT), F32),
        pltpu.VMEM((2, 1, LAT), F32),
        pltpu.VMEM((2, PLANE, 2 * LAT), BF16),
        pltpu.VMEM((2, PLANE, 2 * LAT), BF16),
        pltpu.VMEM((PLANE, 2 * PLANE), BF16),
        pltpu.VMEM((PLANE, 2 * LAT), BF16),
        pltpu.VMEM((PLANE, 2 * LAT), BF16),
        pltpu.VMEM((TILES, NX, NY, NZ * ROWS, TILE), F32),
        pltpu.VMEM((TILES, NX, NY, NZ * ROWS, TILE), BF16),
        pltpu.VMEM((TILES, NY, NZ * ROWS, TILE), F32),
        pltpu.VMEM((TILES, NY, NZ * ROWS, TILE), BF16),
        pltpu.VMEM((NZ, TILES, 16, TILE // 4), BF16),
        pltpu.VMEM((NZ, TILES, 16, TILE // 4), F32),
        pltpu.VMEM((TILES, NY, NZ * ROWS, TILE), BF16),
        pltpu.VMEM((TILES, NY, NZ * ROWS, TILE), BF16),
        pltpu.VMEM((TILES, NY, NX, NZ * ROWS, TILE), BF16),
        pltpu.VMEM((TILES, NZ * ROWS, TILE), BF16),
        pltpu.VMEM((NZ, TILES, 16, TILE // 4), BF16),
        dma((3,)),
        dma((5,)),
        dma((5,)),
        dma((3,)),
        dma((3,)),
        dma((NZ,)),
        dma((NZ,)),
        dma((NZ, NY)),
        dma((NZ, NY)),
        dma((NZ,)),
        dma((NZ,)),
        dma((NZ,)),
        dma((NZ,)),
        dma((NZ, NY)),
        dma((NZ, NY)),
        dma((TILES, NY)),
        dma((TILES, NY)),
        dma((TILES, NY)),
        dma((TILES, NY)),
        dma((len(Z_GROUPS), NZ)),
        dma((len(Z_GROUPS), NZ)),
    ]
    return pl.pallas_call(
        kernel,
        out_shape=jax.ShapeDtypeStruct((1, ROWS, D), BF16),
        in_specs=[vmem, vmem, vmem, vmem, hbm, hbm, hbm],
        out_specs=vmem,
        scratch_shapes=scratch,
        compiler_params=pltpu.CompilerParams(
            collective_id=0, has_side_effects=True, vmem_limit_bytes=58 * 2**20
        ),
    )(
        token_ids.reshape(1, 2 * PLANE),
        resid,
        enc_bias,
        threshold,
        enc_weight,
        dec_self,
        dec_cross,
    )


def solution(mesh):
    in_specs = (
        P("src", "lat", None),
        P(),
        P("src", None, "lat"),
        P("src", "lat"),
        P("src", "lat"),
        P("src", "lat", None),
        P("lat", None),
    )
    out_specs = P("src", "lat", None)
    return jax.shard_map(
        on_device, mesh=mesh, in_specs=in_specs, out_specs=out_specs, check_vma=False
    )
```

time: 914 us -> 79.4 us (0.09)
  blocking collectives: 737 us -> 0 us
  waiting for transfers between devices: 139 us -> 0 us
  Pallas kernels: 0 us -> 77.8 us
  matrix products: 14.4 us -> 0 us
  between operations: 14.1 us -> 0.01 us
    unnamed x1 -> x0, blocking collectives: 737 us -> none
    all_gather x1 -> x0, waiting for transfers between devices: 131 us -> none  [on_device(): lax.all_gather(rows, 'lat', axis=0, tiled=True)]
    pallas_call x0 -> x1, Pallas kernels: none -> 77.8 us  [on_device(): pl.pallas_call(kernel, out_shape=jax.ShapeDtypeStruct((1, ROWS, D), BF16)...]
    dot_general x3 -> x0, matrix products: 14.4 us -> none  [the longest x1 8.61 us: on_device(): jnp.dot(lax.all_gather(rows, 'lat', axis=0, tiled=True), weight, preferre...]
  transfers between devices with their start and end apart: 2 -> 0, of which waited for: 2 -> 0; matrix products, arithmetic and copies ran while one was open for 0% -> 0% of each run, Pallas kernels for 0% -> 0%
where the time goes in v1:
time: 79.4 us; the launch traced here: 79.2 us
  Pallas kernels  77.8 us (98%)
  local copies, waits for them, and re-layouts  1.39 us (2%)
    pallas_call x1, Pallas kernels, on_device(): pl.pallas_call(kernel, out_shape=jax.ShapeDtypeStruct((1, ROWS, D), BF16)...  77.8 us

profile of v1, /device:TPU:2, one launch (start us, length us, event | category | flops | bytes accessed | tf_op | source)
XLA Modules:
  0.0 79.2 jit_solution(4967450569400507595)
XLA Ops:
  0.0 77.8 %shard_map.73 = bf16[1,4,4096]{2,1,0:T(4,128)(2,1)} custom-call(s32[1,512]{1,0:T(1,128)} %bitcast.1, bf16[1,4,4096]{2,1,0:T(4,128)(2,1)} %resid.1, f32[1,256]{1,0:T(1,128)} %bias.1, f32[1,256]{1,0:T(1,128)} %thresh.1, bf16[1,4096,256]{2,1,0:T(8,128)(2,1)} %enc_hbm.1, bf16[1,256,4096]{2,1,0:T(8,128)(2,1)} %own_hbm.1, bf16[256,4096]{1,0:T(8,128)(2,1)} %cross_hbm.1), custom_call_target="tpu_custom_call" | custom-call | tf_op jit(solution)/shard_map/pallas_call | solution.py:498
  77.8 1.4 %copy.9 = bf16[1,4,4096]{2,1,0:T(4,128)(2,1)} copy(bf16[1,4,4096]{2,1,0:T(4,128)(2,1)} %shard_map.73) | data formatting | bytes 65536

commit v2 on v1

v2 whole, which is shorter than its diff:
```python
import jax
import jax.numpy as jnp
from jax import lax
from jax.experimental import pallas as pl
from jax.experimental.pallas import tpu as pltpu
from jax.sharding import PartitionSpec as P

MESH = pl.DeviceIdType.MESH
BF16, F32 = jnp.bfloat16, jnp.float32

NZ, NX, NY = 8, 2, 4
ROWS = 4
D, LAT = 4096, 256
PLANE = NZ * NX * NY * ROWS
QUARTER = D // 4
ZLAST = 256
XFIRST = {0: 384, 1: 256, 2: 384, 3: 256, 4: 384, 5: 256, 6: 384, 7: 256}
TILE = 512
TILES = D // TILE
Z_TILES = 2
Y_TILES = (2, 5)
GROUPS = ((0, 1), (1, 2), (2, 4), (4, 6), (6, 8))
Z_ORDER = (0, 1, 7, 2, 6, 3, 5, 4)
Y_ORDER = (1, 3, 2)
PLANE_ORDER = ((0, 1), (0, 3), (1, 0), (0, 2), (1, 1), (1, 3), (1, 2))


def kernel(
    ids_hbm,
    resid,
    bias,
    thresh,
    enc_hbm,
    own_hbm,
    cross_hbm,
    out,
    blocks,
    rows,
    enc,
    own_dec,
    cross_dec,
    bias2,
    thresh2,
    codes,
    earlier,
    select,
    mixed,
    mixed_cross,
    part,
    send1,
    half,
    send2,
    send3,
    last,
    got_x1,
    got_y2,
    got_y1,
    got_x2,
    got_z,
    got_a,
    got_h,
    row_buf,
    ids_buf,
    local_sem,
    sent,
    core_recv,
    code_recv,
    z_recv,
    cy_recv,
    cx_recv,
    bx_recv,
    by_recv,
    a1_recv,
    az_recv,
    r1_recv,
    r2_recv,
    s1_recv,
    s2_recv,
    s3_recv,
):
    src = lax.axis_index("src")
    lat = lax.axis_index("lat")
    core = lax.rem(lat, 2)
    y = lax.rem(lat // 2, NY)
    x = lax.rem(lat // (2 * NY), NX)
    z = lat // (2 * NY * NX)

    def at(z, x, y, core):
        return (src, ((z * NX + x) * NY + y) * 2 + core)

    def zp(dz):
        return lax.rem(z + NZ - dz, NZ)

    def zn(dz):
        return lax.rem(z + dz, NZ)

    def xn(dx):
        return lax.rem(x + dx, NX)

    def yn(dy):
        return lax.rem(y + dy, NY)

    other_core = at(z, x, y, 1 - core)
    other_src = (1 - src, lat)
    other_x = at(z, 1 - x, y, core)

    def remote(src_ref, dst_ref, recv, device):
        return pltpu.make_async_remote_copy(
            src_ref=src_ref,
            dst_ref=dst_ref,
            send_sem=sent,
            recv_sem=recv,
            device_id=device,
            device_id_type=MESH,
        )

    def arrived(ref, recv):
        remote(ref, ref, recv, other_core).wait_recv()

    started = []

    def go(make, *args):
        make(*args).start()
        started.append((make, args))

    locals_ = [
        pltpu.make_async_copy(enc_hbm.at[0], enc.at[core], local_sem.at[0]),
        pltpu.make_async_copy(own_hbm.at[0], own_dec.at[core], local_sem.at[1]),
        pltpu.make_async_copy(cross_hbm, cross_dec.at[core], local_sem.at[2]),
        pltpu.make_async_copy(resid.at[0], row_buf, local_sem.at[3]),
        pltpu.make_async_copy(ids_hbm, ids_buf, local_sem.at[4]),
        pltpu.make_async_copy(bias, bias2.at[core], local_sem.at[5]),
        pltpu.make_async_copy(thresh, thresh2.at[core], local_sem.at[6]),
    ]
    for n in (3, 4, 5, 6, 0, 1, 2):
        locals_[n].start()

    barrier = pltpu.get_barrier_semaphore()
    peers = [at(zn(o), x, y, core) for o in range(1, NZ)]
    peers += [at(z, xn(dx), yn(dy), core) for dx, dy in PLANE_ORDER]
    peers += [other_core, other_src]
    for peer in peers:
        pl.semaphore_signal(barrier, inc=1, device_id=peer, device_id_type=MESH)

    locals_[3].wait()
    mine = row_buf[...].astype(F32)
    blocks[z, x, y] = jnp.concatenate(
        [mine[:, q * QUARTER : (q + 1) * QUARTER] for q in range(4)], axis=0
    ).astype(BF16)

    pl.semaphore_wait(barrier, len(peers))

    a_cols, z_cols = pl.ds(0, ZLAST), pl.ds(ZLAST, QUARTER - ZLAST)

    def b_cols(dz):
        return pl.ds(ZLAST, XFIRST[dz])

    def c_cols(dz):
        return pl.ds(ZLAST + XFIRST[dz], QUARTER - ZLAST - XFIRST[dz])

    def same(ref, recv, device):
        return remote(ref, ref, recv, device)

    def z_copy(o):
        ref = blocks.at[z, x, y, :, z_cols]
        return same(ref, z_recv.at[o], at(zn(o), x, y, core))

    def a1_copy(dx, dy):
        ref = blocks.at[z, x, y, :, a_cols]
        peer = at(z, xn(dx), yn(dy), core)
        return same(ref, a1_recv.at[0], peer)

    def az_copy(n):
        dz, o = ((0, 1), (0, 7), (0, 2), (0, 6), (2, 1), (6, 7), (2, 2), (6, 6))[n]
        xs = slice(None) if n < 6 else n - 6
        ref = blocks.at[zp(dz), xs, :, :, a_cols]
        return same(ref, az_recv.at[n], at(zn(o), x, y, core))

    AZ_OF = {1: (0,), 7: (1,), 2: (2,), 6: (3,), 3: (4,), 5: (5,), 4: (6, 7)}

    def cy_copy(dz, o):
        ref = blocks.at[zp(dz), x, y, :, c_cols(dz)]
        return same(ref, cy_recv.at[dz], at(z, x, yn(o), core))

    def bx_copy(dz):
        ref = blocks.at[zp(dz), x, y, :, b_cols(dz)]
        return same(ref, bx_recv.at[dz], other_x)

    def cx_copy(dz):
        ref = blocks.at[zp(dz), x, :, :, c_cols(dz)]
        return same(ref, cx_recv.at[dz], other_x)

    def by_copy(dz, o):
        ref = blocks.at[zp(dz), :, y, :, b_cols(dz)]
        return same(ref, by_recv.at[dz], at(z, x, yn(o), core))

    def second(dz):
        if dz:
            z_copy(dz).wait_recv()
        for o in Y_ORDER:
            go(cy_copy, dz, o)
        go(bx_copy, dz)

    def third(dz):
        bx_copy(dz).wait_recv()
        for o in Y_ORDER:
            go(by_copy, dz, o)
        arrived(blocks.at[zp(dz), x, pl.ds(0, 3), :, c_cols(dz)], cy_recv.at[dz])
        go(cx_copy, dz)

    def plane_done():
        arrived(blocks.at[pl.ds(0, 7), x, y, :, a_cols], a1_recv.at[0])
        for n in range(4):
            go(az_copy, n)

    def pass_on():
        for dz in (2, 6):
            for n in AZ_OF[dz]:
                az_copy(n).wait_recv()
            go(az_copy, 4 if dz == 2 else 5)
            go(az_copy, 6 if dz == 2 else 7)

    for o in Z_ORDER[1:]:
        go(z_copy, o)
    for dx, dy in PLANE_ORDER:
        go(a1_copy, dx, dy)
    second(0)

    def core_copy(n):
        src_ref, dst_ref = (
            (bias, bias2.at[core]),
            (thresh, thresh2.at[core]),
            (enc_hbm.at[0], enc.at[core]),
            (own_hbm.at[0], own_dec.at[core]),
            (cross_hbm, cross_dec.at[core]),
        )[n]
        return remote(src_ref, dst_ref, core_recv.at[n], other_core)

    for n in range(4):
        go(core_copy, n)

    @pl.when(src == 1)
    def _():
        core_copy(4).start()

    locals_[4].wait()
    shape = (2 * PLANE, 2 * PLANE)
    j = lax.broadcasted_iota(jnp.int32, shape, 0)
    plane, within = j // PLANE, j % PLANE
    pool = (within // ROWS) * (2 * ROWS) + plane * ROWS + within % ROWS
    named = (jnp.broadcast_to(ids_buf[...], shape) == pool).astype(F32).astype(BF16)
    i = lax.broadcasted_iota(jnp.int32, shape, 0)
    t = lax.broadcasted_iota(jnp.int32, shape, 1)
    ir, iz, ixy = i % ROWS, (i // ROWS) % NZ, (i // (ROWS * NZ)) % (NX * NY)
    token = jnp.where(
        i < PLANE,
        (iz * NX * NY + ixy) * (2 * ROWS) + core * ROWS + ir,
        ((i - PLANE) // ROWS) * (2 * ROWS) + core * ROWS + ir,
    )
    order = (t == token).astype(F32).astype(BF16)
    select[...] = lax.dot_general(
        order, named, (((1,), (1,)), ((), ())), preferred_element_type=F32
    ).astype(BF16)

    second(1)
    second(7)
    plane_done()
    second(2)
    third(0)
    second(6)
    third(1)
    second(3)
    third(7)
    second(5)
    third(2)
    second(4)
    pass_on()
    third(6)
    third(3)
    third(5)
    third(4)

    def unpack(dz):
        zz = zp(dz)
        for xx in range(NX):
            four = [blocks[zz, xx, yy].astype(F32) for yy in range(NY)]
            start = pl.multiple_of((zz * NX + xx) * (NY * ROWS), NY * ROWS)
            for q in range(4):
                rows[pl.ds(start, NY * ROWS), q * QUARTER : (q + 1) * QUARTER] = (
                    jnp.concatenate([b[4 * q : 4 * q + 4] for b in four], axis=0)
                ).astype(BF16)

    for dz in Z_ORDER:
        for n in AZ_OF.get(dz, ()):
            if n not in AZ_OF[2] + AZ_OF[6]:
                az_copy(n).wait_recv()
        arrived(blocks.at[zp(dz), :, pl.ds(0, 3), :, b_cols(dz)], by_recv.at[dz])
        cx_copy(dz).wait_recv()
        unpack(dz)

    def code_copy(h):
        ref = codes.at[h, core]
        return same(ref, code_recv.at[0, h], other_core)

    def over_copy(h):
        return remote(
            codes.at[h, core],
            earlier.at[h, core],
            code_recv.at[1, h],
            other_src,
        )

    def on_copy(h):
        ref = earlier.at[h, core]
        return same(ref, code_recv.at[2, h], other_core)

    for n in (0, 5, 6):
        locals_[n].wait()
    for n in range(3):
        core_copy(n).wait_recv()
    for h in range(2):
        pre = jnp.dot(rows[...], enc[h], preferred_element_type=F32) + bias2[h]
        gate = jnp.clip((pre - thresh2[h]) / 0.1, 0.0, 1.0)
        codes[h, core] = (pre * gate).astype(BF16)

        @pl.when(src == 0)
        def _():
            over_copy(h).start()

        go(code_copy, h)

    def permute(ref, into, h):
        into[:, h * LAT : (h + 1) * LAT] = jnp.dot(
            select[...], ref[h].reshape(2 * PLANE, LAT), preferred_element_type=F32
        ).astype(BF16)

    for h in range(2):
        code_copy(h).wait_recv()
        permute(codes, mixed, h)
    locals_[1].wait()
    core_copy(3).wait_recv()
    locals_[2].wait()

    def product(left, right, n):
        start = PLANE if n < Z_TILES else 0
        return sum(
            jnp.dot(
                left[start : start + PLANE, h * LAT : (h + 1) * LAT],
                right[h, :, n * TILE : (n + 1) * TILE],
                preferred_element_type=F32,
            )
            for h in range(2)
        ).reshape(NX, NY, NZ * ROWS, TILE)

    def y1_copy(n, o):
        return remote(
            send1.at[n, :, yn(o)],
            got_y1.at[n, o],
            s1_recv.at[n],
            at(z, x, yn(o), core),
        )

    def x1_copy(n):
        return remote(
            send1.at[n, 1 - x], got_x1.at[n], s1_recv.at[n], other_x
        )

    def y2_copy(n, o):
        return remote(
            send2.at[n, yn(o)],
            got_y2.at[n, o],
            s2_recv.at[n],
            at(z, x, yn(o), core),
        )

    def x2_copy(n):
        return remote(
            send2.at[n, 1 - x], got_x2.at[n], s2_recv.at[n], other_x
        )

    def r1_copy(n, k):
        o, to, first, count = (
            (1, 1, 0, 32),
            (7, 7, 0, 32),
            (3, 1, 0, 32),
            (5, 7, 0, 32),
            (4, 2, 0, 16),
            (4, 6, 16, 16),
        )[k]
        zz = zn(o)
        return remote(
            send1.at[n, zz // NY, zz % NY, pl.ds(first, count)],
            got_a.at[n, k] if k < 4 else got_h.at[n, k - 4],
            r1_recv.at[n, k],
            at(zn(to), x, y, core),
        )

    def r2_copy(n, k):
        return remote(
            send2.at[n, k],
            got_a.at[n, 4 + k],
            r2_recv.at[n, k],
            at(zn((2, 6)[k]), x, y, core),
        )

    def last_copy(g, k):
        first, end = GROUPS[g]
        tiles = pl.ds(first, end - first)
        if first < Z_TILES:
            xx, yy = xn(k // NY), yn(k % NY)
            peer, place = at(z, xx, yy, core), xx * NY + yy
        else:
            peer, place = at(zn(k), x, y, core), zn(k)
        return remote(
            send3.at[place, tiles],
            got_z.at[k, tiles],
            s3_recv.at[g],
            peer,
        )

    def first_copies(n):
        if n < Z_TILES:
            return [(r1_copy, (n, k)) for k in (4, 5, 2, 3, 0, 1)]
        if n in Y_TILES:
            return [(y1_copy, (n, o)) for o in Y_ORDER]
        return [(x1_copy, (n,))]

    def stage1(n, total):
        send1[n] = total.astype(BF16)
        for make, args in first_copies(n):
            make(*args).start()

    def stage2(n):
        if n < Z_TILES:
            for k in (2, 3, 4, 5):
                r1_copy(n, k).wait_recv()
            for k in range(2):
                zz = zn((2, 6)[k])
                total = part[n, zz // NY, zz % NY] + got_a[n, 2 + k].astype(F32)
                more = got_h[n, k].astype(F32)
                top, low = total[:16], total[16:]
                if k == 0:
                    top += more
                else:
                    low += more
                send2[n, k, 0:16] = top.astype(BF16)
                send2[n, k, 16:32] = low.astype(BF16)
                go(r2_copy, n, k)
        elif n in Y_TILES:
            total = part[n, :, y]
            arrived(got_y1.at[n, pl.ds(1, 3)], s1_recv.at[n])
            for o in Y_ORDER:
                total += got_y1[n, o].astype(F32)
            half[n, 0:NX] = total
            send2[n, 0:NX] = total.astype(BF16)
            go(x2_copy, n)
        else:
            x1_copy(n).wait_recv()
            total = part[n, x] + got_x1[n].astype(F32)
            half[n] = total
            send2[n] = total.astype(BF16)
            for o in Y_ORDER:
                go(y2_copy, n, o)

    def stage3(n):
        if n < Z_TILES:
            total = part[n, z // NY, z % NY]
            for k in range(2):
                r1_copy(n, k).wait_recv()
                total += got_a[n, k].astype(F32)
            for k in range(2):
                r2_copy(n, k).wait_recv()
                total += got_a[n, 4 + k].astype(F32)
        elif n in Y_TILES:
            x2_copy(n).wait_recv()
            total = half[n, x] + got_x2[n].astype(F32)
        else:
            total = half[n, y]
            arrived(got_y2.at[n, pl.ds(1, 3)], s2_recv.at[n])
            for o in Y_ORDER:
                total += got_y2[n, o].astype(F32)
        step = TILE // 4
        for k in range(8):
            block = jnp.concatenate(
                [
                    total[k * ROWS : (k + 1) * ROWS, q * step : (q + 1) * step]
                    for q in range(4)
                ],
                axis=0,
            )
            last[k, n] = block
            send3[k, n] = block.astype(BF16)
        for g, (_, end) in enumerate(GROUPS):
            if n == end - 1:
                for k in (4, 3, 5, 2, 6, 1, 7):
                    go(last_copy, g, k)

    def finish(g):
        first, end = GROUPS[g]
        arrived(got_z.at[pl.ds(1, 7), pl.ds(first, end - first)], s3_recv.at[g])
        step = TILE // 4
        for n in range(first, end):
            total = last[x * NY + y if n < Z_TILES else z, n]
            for k in range(1, 8):
                total += got_z[k, n].astype(F32)
            for q in range(4):
                out[0, :, n * TILE + q * step : n * TILE + (q + 1) * step] = total[
                    q * ROWS : (q + 1) * ROWS
                ].astype(BF16)

    for n in range(TILES):
        started.extend(first_copies(n))
        part[n] = product(mixed, own_dec, n)

        @pl.when(src == 0)
        def _():
            stage1(n, part[n])

    @pl.when(src == 1)
    def _():
        core_copy(4).wait_recv()
        for h in range(2):
            over_copy(h).wait_recv()
            on_copy(h).start()
        for h in range(2):
            on_copy(h).wait_recv()
            permute(earlier, mixed_cross, h)
        for n in range(TILES):
            total = part[n] + product(mixed_cross, cross_dec, n)
            part[n] = total
            stage1(n, total)

    for n in range(TILES + 2):
        if n < TILES:
            stage2(n)
        if n >= 2:
            stage3(n - 2)
    for g in range(len(GROUPS)):
        finish(g)

    for make, args in started:
        make(*args).wait_send()

    @pl.when(src == 0)
    def _():
        for h in range(2):
            over_copy(h).wait_send()

    @pl.when(src == 1)
    def _():
        core_copy(4).wait_send()
        for h in range(2):
            on_copy(h).wait_send()


def on_device(
    resid, token_ids, enc_weight, enc_bias, threshold, dec_self, dec_cross
):
    vmem = pl.BlockSpec(memory_space=pltpu.VMEM)
    hbm = pl.BlockSpec(memory_space=pl.ANY)
    dma = pltpu.SemaphoreType.DMA
    scratch = [
        pltpu.VMEM((NZ, NX, NY, 16, QUARTER), BF16),
        pltpu.VMEM((PLANE, D), BF16),
        pltpu.VMEM((2, D, LAT), BF16),
        pltpu.VMEM((2, LAT, D), BF16),
        pltpu.VMEM((2, LAT, D), BF16),
        pltpu.VMEM((2, 1, LAT), F32),
        pltpu.VMEM((2, 1, LAT), F32),
        pltpu.VMEM((2, 2, PLANE, LAT), BF16),
        pltpu.VMEM((2, 2, PLANE, LAT), BF16),
        pltpu.VMEM((2 * PLANE, 2 * PLANE), BF16),
        pltpu.VMEM((2 * PLANE, 2 * LAT), BF16),
        pltpu.VMEM((2 * PLANE, 2 * LAT), BF16),
        pltpu.VMEM((TILES, NX, NY, NZ * ROWS, TILE), F32),
        pltpu.VMEM((TILES, NX, NY, NZ * ROWS, TILE), BF16),
        pltpu.VMEM((TILES, NY, NZ * ROWS, TILE), F32),
        pltpu.VMEM((TILES, NY, NZ * ROWS, TILE), BF16),
        pltpu.VMEM((NZ, TILES, 16, TILE // 4), BF16),
        pltpu.VMEM((NZ, TILES, 16, TILE // 4), F32),
        pltpu.VMEM((TILES, NY, NZ * ROWS, TILE), BF16),
        pltpu.VMEM((TILES, NY, NZ * ROWS, TILE), BF16),
        pltpu.VMEM((TILES, NY, NX, NZ * ROWS, TILE), BF16),
        pltpu.VMEM((TILES, NZ * ROWS, TILE), BF16),
        pltpu.VMEM((NZ, TILES, 16, TILE // 4), BF16),
        pltpu.VMEM((Z_TILES, 6, NZ * ROWS, TILE), BF16),
        pltpu.VMEM((Z_TILES, 2, 16, TILE), BF16),
        pltpu.VMEM((ROWS, D), BF16),
        pltpu.VMEM((1, 2 * PLANE), jnp.int32),
        dma((7,)),
        dma,
        dma((5,)),
        dma((3, 2)),
        dma((NZ,)),
        dma((NZ,)),
        dma((NZ,)),
        dma((NZ,)),
        dma((NZ,)),
        dma((1,)),
        dma((8,)),
        dma((Z_TILES, 6)),
        dma((Z_TILES, 2)),
        dma((TILES,)),
        dma((TILES,)),
        dma((len(GROUPS),)),
    ]
    return pl.pallas_call(
        kernel,
        out_shape=jax.ShapeDtypeStruct((1, ROWS, D), BF16),
        in_specs=[hbm] * 7,
        out_specs=vmem,
        scratch_shapes=scratch,
        compiler_params=pltpu.CompilerParams(
            collective_id=0, has_side_effects=True, vmem_limit_bytes=58 * 2**20
        ),
    )(
        token_ids.reshape(1, 2 * PLANE),
        resid,
        enc_bias,
        threshold,
        enc_weight,
        dec_self,
        dec_cross,
    )


def solution(mesh):
    in_specs = (
        P("src", "lat", None),
        P(),
        P("src", None, "lat"),
        P("src", "lat"),
        P("src", "lat"),
        P("src", "lat", None),
        P("lat", None),
    )
    out_specs = P("src", "lat", None)
    return jax.shard_map(
        on_device, mesh=mesh, in_specs=in_specs, out_specs=out_specs, check_vma=False
    )
```

time: 79.4 us -> 66.1 us (0.83)
  the two profiles are of different devices: /device:TPU:2 before, /device:TPU:6 now
where the time goes in v2:
time: 66.1 us; the launch traced here: 65.9 us
  Pallas kernels  64.5 us (98%)
  local copies, waits for them, and re-layouts  1.39 us (2%)
    pallas_call x1, Pallas kernels, on_device(): pl.pallas_call(kernel, out_shape=jax.ShapeDtypeStruct((1, ROWS, D), BF16)...  64.5 us
    unnamed x1, local copies, waits for them, and re-layouts  1.39 us

profile of v2, /device:TPU:6, one launch (start us, length us, event | category | flops | bytes accessed | tf_op | source)
XLA Modules:
  0.0 65.9 jit_solution(7683656603386179913)
XLA Ops:
  0.0 64.5 %shard_map.73 = bf16[1,4,4096]{2,1,0:T(4,128)(2,1)} custom-call(s32[1,512]{1,0:T(1,128)} %bitcast.1, bf16[1,4,4096]{2,1,0:T(4,128)(2,1)} %resid.1, f32[1,256]{1,0:T(1,128)} %bias.1, f32[1,256]{1,0:T(1,128)} %thresh.1, bf16[1,4096,256]{2,1,0:T(8,128)(2,1)} %enc_hbm.1, bf16[1,256,4096]{2,1,0:T(8,128)(2,1)} %own_hbm.1, bf16[256,4096]{1,0:T(8,128)(2,1)} %cross_hbm.1), custom_call_target="tpu_custom_call" | custom-call | tf_op jit(solution)/shard_map/pallas_call | solution.py:607
  64.5 1.4 %copy.9 = bf16[1,4,4096]{2,1,0:T(4,128)(2,1)} copy(bf16[1,4,4096]{2,1,0:T(4,128)(2,1)} %shard_map.73) | data formatting | bytes 65536

commit v3 on v2

--- a/solution.py
+++ b/solution.py
@@ -14,14 +14,17 @@
 PLANE = NZ * NX * NY * ROWS
 QUARTER = D // 4
 ZLAST = 256
-XFIRST = {0: 384, 1: 256, 2: 384, 3: 256, 4: 384, 5: 256, 6: 384, 7: 256}
+XFIRST = {i: 384 for i in range(8)}
 TILE = 512
 TILES = D // TILE
 Z_TILES = 2
-Y_TILES = (2, 5)
+Y_TILES = (2, 4, 6)
 GROUPS = ((0, 1), (1, 2), (2, 4), (4, 6), (6, 8))
 Z_ORDER = (0, 1, 7, 2, 6, 3, 5, 4)
 Y_ORDER = (1, 3, 2)
+TILE_ORDER = (2, 3, 0, 4, 5, 1, 6, 7)
+LAG = 4
+PARTS = ((0, 5), (5, 8))
 PLANE_ORDER = ((0, 1), (0, 3), (1, 0), (0, 2), (1, 1), (1, 3), (1, 2))
 
 
@@ -247,7 +250,10 @@
     shape = (2 * PLANE, 2 * PLANE)
     j = lax.broadcasted_iota(jnp.int32, shape, 0)
     plane, within = j // PLANE, j % PLANE
-    pool = (within // ROWS) * (2 * ROWS) + plane * ROWS + within % ROWS
+    step = within // (NX * NY * ROWS)
+    far = jnp.where(step % 2 == 0, step // 2, NZ - (step + 1) // 2)
+    pool = (z + far) % NZ * (NX * NY) + (within // ROWS) % (NX * NY)
+    pool = pool * (2 * ROWS) + plane * ROWS + within % ROWS
     named = (jnp.broadcast_to(ids_buf[...], shape) == pool).astype(F32).astype(BF16)
     i = lax.broadcasted_iota(jnp.int32, shape, 0)
     t = lax.broadcasted_iota(jnp.int32, shape, 1)
@@ -266,76 +272,87 @@
     second(7)
     plane_done()
     second(2)
+    second(6)
     third(0)
-    second(6)
+    second(3)
+    second(5)
     third(1)
-    second(3)
     third(7)
-    second(5)
-    third(2)
     second(4)
     pass_on()
+    third(2)
     third(6)
     third(3)
     third(5)
     third(4)
 
-    def unpack(dz):
+    def unpack(place, dz):
         zz = zp(dz)
         for xx in range(NX):
             four = [blocks[zz, xx, yy].astype(F32) for yy in range(NY)]
-            start = pl.multiple_of((zz * NX + xx) * (NY * ROWS), NY * ROWS)
+            start = (place * NX + xx) * (NY * ROWS)
             for q in range(4):
-                rows[pl.ds(start, NY * ROWS), q * QUARTER : (q + 1) * QUARTER] = (
+                rows[start : start + NY * ROWS, q * QUARTER : (q + 1) * QUARTER] = (
                     jnp.concatenate([b[4 * q : 4 * q + 4] for b in four], axis=0)
                 ).astype(BF16)
 
-    for dz in Z_ORDER:
-        for n in AZ_OF.get(dz, ()):
-            if n not in AZ_OF[2] + AZ_OF[6]:
-                az_copy(n).wait_recv()
-        arrived(blocks.at[zp(dz), :, pl.ds(0, 3), :, b_cols(dz)], by_recv.at[dz])
-        cx_copy(dz).wait_recv()
-        unpack(dz)
-
-    def code_copy(h):
-        ref = codes.at[h, core]
-        return same(ref, code_recv.at[0, h], other_core)
-
-    def over_copy(h):
-        return remote(
-            codes.at[h, core],
-            earlier.at[h, core],
-            code_recv.at[1, h],
+    def bounds(c):
+        first, end = PARTS[c]
+        return first * NX * NY * ROWS, (end - first) * NX * NY * ROWS
+
+    def code_copy(c):
+        ref = codes.at[:, core, pl.ds(*bounds(c))]
+        return same(ref, code_recv.at[0, c], other_core)
+
+    def over_copy(c):
+        return remote(
+            codes.at[:, core, pl.ds(*bounds(c))],
+            earlier.at[:, core, pl.ds(*bounds(c))],
+            code_recv.at[1, c],
             other_src,
         )
 
-    def on_copy(h):
-        ref = earlier.at[h, core]
-        return same(ref, code_recv.at[2, h], other_core)
-
-    for n in (0, 5, 6):
-        locals_[n].wait()
-    for n in range(3):
-        core_copy(n).wait_recv()
-    for h in range(2):
-        pre = jnp.dot(rows[...], enc[h], preferred_element_type=F32) + bias2[h]
-        gate = jnp.clip((pre - thresh2[h]) / 0.1, 0.0, 1.0)
-        codes[h, core] = (pre * gate).astype(BF16)
+    def on_copy(c):
+        ref = earlier.at[:, core, pl.ds(*bounds(c))]
+        return same(ref, code_recv.at[2, c], other_core)
+
+    for c, (first, end) in enumerate(PARTS):
+        for place in range(first, end):
+            dz = Z_ORDER[place]
+            for n in AZ_OF.get(dz, ()):
+                if n not in AZ_OF[2] + AZ_OF[6]:
+                    az_copy(n).wait_recv()
+            arrived(blocks.at[zp(dz), :, pl.ds(0, 3), :, b_cols(dz)], by_recv.at[dz])
+            cx_copy(dz).wait_recv()
+            unpack(place, dz)
+        if c == 0:
+            for n in (0, 5, 6):
+                locals_[n].wait()
+            for n in range(3):
+                core_copy(n).wait_recv()
+        start, count = bounds(c)
+        for h in range(2):
+            pre = jnp.dot(
+                rows[start : start + count], enc[h], preferred_element_type=F32
+            )
+            pre += bias2[h]
+            gate = jnp.clip((pre - thresh2[h]) / 0.1, 0.0, 1.0)
+            codes[h, core, start : start + count] = (pre * gate).astype(BF16)
 
         @pl.when(src == 0)
         def _():
-            over_copy(h).start()
-
-        go(code_copy, h)
+            over_copy(c).start()
+
+        go(code_copy, c)
 
     def permute(ref, into, h):
         into[:, h * LAT : (h + 1) * LAT] = jnp.dot(
             select[...], ref[h].reshape(2 * PLANE, LAT), preferred_element_type=F32
         ).astype(BF16)
 
+    for c in range(2):
+        code_copy(c).wait_recv()
     for h in range(2):
-        code_copy(h).wait_recv()
         permute(codes, mixed, h)
     locals_[1].wait()
     core_copy(3).wait_recv()
@@ -508,7 +525,7 @@
                     q * ROWS : (q + 1) * ROWS
                 ].astype(BF16)
 
-    for n in range(TILES):
+    for n in TILE_ORDER:
         started.extend(first_copies(n))
         part[n] = product(mixed, own_dec, n)
 
@@ -519,22 +536,23 @@
     @pl.when(src == 1)
     def _():
         core_copy(4).wait_recv()
+        for c in range(2):
+            over_copy(c).wait_recv()
+            on_copy(c).start()
+        for c in range(2):
+            on_copy(c).wait_recv()
         for h in range(2):
-            over_copy(h).wait_recv()
-            on_copy(h).start()
-        for h in range(2):
-            on_copy(h).wait_recv()
             permute(earlier, mixed_cross, h)
-        for n in range(TILES):
+        for n in TILE_ORDER:
             total = part[n] + product(mixed_cross, cross_dec, n)
             part[n] = total
             stage1(n, total)
 
-    for n in range(TILES + 2):
+    for n in range(TILES + LAG):
         if n < TILES:
             stage2(n)
-        if n >= 2:
-            stage3(n - 2)
+        if n >= LAG:
+            stage3(n - LAG)
     for g in range(len(GROUPS)):
         finish(g)
 

time: 66.1 us -> 57.6 us (0.87)
  the two profiles are of different devices: /device:TPU:6 before, /device:TPU:2 now
where the time goes in v3:
time: 57.6 us; the launch traced here: 57.5 us
  Pallas kernels  56.1 us (97%)
  local copies, waits for them, and re-layouts  1.39 us (2%)
    pallas_call x1, Pallas kernels, on_device(): pl.pallas_call(kernel, out_shape=jax.ShapeDtypeStruct((1, ROWS, D), BF16)...  56.1 us
    unnamed x1, local copies, waits for them, and re-layouts  1.39 us

profile of v3, /device:TPU:2, one launch (start us, length us, event | category | flops | bytes accessed | tf_op | source)
XLA Modules:
  0.0 57.5 jit_solution(15353242644933880017)
XLA Ops:
  0.0 56.1 %shard_map.73 = bf16[1,4,4096]{2,1,0:T(4,128)(2,1)} custom-call(s32[1,512]{1,0:T(1,128)} %bitcast.1, bf16[1,4,4096]{2,1,0:T(4,128)(2,1)} %resid.1, f32[1,256]{1,0:T(1,128)} %bias.1, f32[1,256]{1,0:T(1,128)} %thresh.1, bf16[1,4096,256]{2,1,0:T(8,128)(2,1)} %enc_hbm.1, bf16[1,256,4096]{2,1,0:T(8,128)(2,1)} %own_hbm.1, bf16[256,4096]{1,0:T(8,128)(2,1)} %cross_hbm.1), custom_call_target="tpu_custom_call" | custom-call | tf_op jit(solution)/shard_map/pallas_call | solution.py:625
  56.1 1.4 %copy.9 = bf16[1,4,4096]{2,1,0:T(4,128)(2,1)} copy(bf16[1,4,4096]{2,1,0:T(4,128)(2,1)} %shard_map.73) | data formatting | bytes 65536

commit v4 on v3

--- a/solution.py
+++ b/solution.py
@@ -24,7 +24,7 @@
 Y_ORDER = (1, 3, 2)
 TILE_ORDER = (2, 3, 0, 4, 5, 1, 6, 7)
 LAG = 4
-PARTS = ((0, 5), (5, 8))
+PARTS = ((0, 4), (4, 7), (7, 8))
 PLANE_ORDER = ((0, 1), (0, 3), (1, 0), (0, 2), (1, 1), (1, 3), (1, 2))
 
 
@@ -350,7 +350,7 @@
             select[...], ref[h].reshape(2 * PLANE, LAT), preferred_element_type=F32
         ).astype(BF16)
 
-    for c in range(2):
+    for c in range(len(PARTS)):
         code_copy(c).wait_recv()
     for h in range(2):
         permute(codes, mixed, h)
@@ -536,10 +536,10 @@
     @pl.when(src == 1)
     def _():
         core_copy(4).wait_recv()
-        for c in range(2):
+        for c in range(len(PARTS)):
             over_copy(c).wait_recv()
             on_copy(c).start()
-        for c in range(2):
+        for c in range(len(PARTS)):
             on_copy(c).wait_recv()
         for h in range(2):
             permute(earlier, mixed_cross, h)
@@ -561,13 +561,13 @@
 
     @pl.when(src == 0)
     def _():
-        for h in range(2):
+        for h in range(len(PARTS)):
             over_copy(h).wait_send()
 
     @pl.when(src == 1)
     def _():
         core_copy(4).wait_send()
-        for h in range(2):
+        for h in range(len(PARTS)):
             on_copy(h).wait_send()
 
 
@@ -608,7 +608,7 @@
         dma((7,)),
         dma,
         dma((5,)),
-        dma((3, 2)),
+        dma((3, len(PARTS))),
         dma((NZ,)),
         dma((NZ,)),
         dma((NZ,)),

time: 57.6 us -> 57.5 us (level)
  no operation moved by 1% of the time
where the time goes in v4:
time: 57.5 us; the launch traced here: 57.4 us
  Pallas kernels  56 us (97%)
  local copies, waits for them, and re-layouts  1.39 us (2%)
    pallas_call x1, Pallas kernels, on_device(): pl.pallas_call(kernel, out_shape=jax.ShapeDtypeStruct((1, ROWS, D), BF16)...  56 us
    unnamed x1, local copies, waits for them, and re-layouts  1.39 us

profile of v4, /device:TPU:2, one launch (start us, length us, event | category | flops | bytes accessed | tf_op | source)
XLA Modules:
  0.0 57.4 jit_solution(1320020005346348257)
XLA Ops:
  0.0 56.0 %shard_map.73 = bf16[1,4,4096]{2,1,0:T(4,128)(2,1)} custom-call(s32[1,512]{1,0:T(1,128)} %bitcast.1, bf16[1,4,4096]{2,1,0:T(4,128)(2,1)} %resid.1, f32[1,256]{1,0:T(1,128)} %bias.1, f32[1,256]{1,0:T(1,128)} %thresh.1, bf16[1,4096,256]{2,1,0:T(8,128)(2,1)} %enc_hbm.1, bf16[1,256,4096]{2,1,0:T(8,128)(2,1)} %own_hbm.1, bf16[256,4096]{1,0:T(8,128)(2,1)} %cross_hbm.1), custom_call_target="tpu_custom_call" | custom-call | tf_op jit(solution)/shard_map/pallas_call | solution.py:625
  56.0 1.4 %copy.9 = bf16[1,4,4096]{2,1,0:T(4,128)(2,1)} copy(bf16[1,4,4096]{2,1,0:T(4,128)(2,1)} %shard_map.73) | data formatting | bytes 65536
